TPU v7x, 32 devices: a whole 2x2x4 slice. The times are simulated.
32 devices in a mesh: grp: 8 (over y, x, core), blk: 4 (over z).
Axes of the slice: x: 2, y: 2, z: 4, core: 2. Of those that a mesh axis runs over, the one named last changes fastest.
Arguments:
- pixels: bfloat16 [32, 65536], P(None, ('grp', 'blk')), may hold values from -6 to 6
- landmark_index: int32 [1, 4096], P(None, ('grp', 'blk')), may hold values from 0 to 2047
- counts: int32 [1, 32], P(None, ('grp', 'blk')), may hold values from 64 to 128, as said below
- factor: bfloat16 [64, 4096], P(None, ('grp', 'blk')), may hold values from -6 to 6
Outputs:
- embedding: float32 [64, 65536], P(None, ('grp', 'blk'))
- log_degree: float32 [1, 65536], P(None, ('grp', 'blk'))
Inputs may be any that keep to these rules, and one draw needn't show every extreme that they name: `landmark_index`: landmark slots of one device point at that device's own pixels. `counts`: some device has all 128 slots live in every draw.
All inputs are finite; a program needn't handle non-finite values.
Results may differ from a plain program's by a relative error of at most 0.0042.
Values may be sent and summed in bfloat16 or wider, within the bound.
A program may use at most 64 MiB of HBM per device.

v0:
```python
import jax
import jax.numpy as jnp
from jax import lax
from jax.sharding import PartitionSpec as P

LAYERS = 32


def per_device(pixels, landmark_index, counts, factor):
    slot_cap = landmark_index.shape[1]
    pix_cols = pixels.shape[1]
    land = jnp.take(pixels, landmark_index[0], axis=1)
    pix_sq = jnp.sum(jnp.square(pixels.astype(jnp.float32)), axis=0, keepdims=True)

    def block_terms(land_blk, fac_blk, mask_blk):
        cross = lax.dot_general(
            land_blk, pixels, (((0,), (0,)), ((), ())), preferred_element_type=jnp.float32
        )
        land_sq = jnp.sum(jnp.square(land_blk.astype(jnp.float32)), axis=0)[:, None]
        dist = land_sq + pix_sq - 2.0 * cross
        kern = jnp.where(mask_blk, jnp.exp(-(2.0 / LAYERS) * dist), 0.0).astype(jnp.bfloat16)
        emb_add = jnp.dot(fac_blk, kern, preferred_element_type=jnp.float32)
        deg_add = jnp.sum(kern.astype(jnp.float32), axis=0, keepdims=True)
        return (emb_add, deg_add)

    emb_sum = jnp.zeros((factor.shape[0], pix_cols), jnp.float32)
    deg_sum = jnp.zeros((1, pix_cols), jnp.float32)
    land_part = lax.all_gather(land, ("grp", "blk"), axis=1, tiled=True)
    fac_part = lax.all_gather(factor, ("grp", "blk"), axis=1, tiled=True)
    cnt_part = lax.all_gather(counts, ("grp", "blk"), axis=1, tiled=True)
    columns = land_part.shape[1]
    live_mask = jnp.arange(slot_cap)[None, :] < cnt_part[0][:, None]
    live_mask = live_mask.reshape(columns, 1)
    live = jnp.sum(cnt_part.astype(jnp.float32))
    block = 256

    def turn(which, sums):
        land_blk = lax.dynamic_slice_in_dim(land_part, which * block, block, 1)
        fac_blk = lax.dynamic_slice_in_dim(fac_part, which * block, block, 1)
        mask_blk = lax.dynamic_slice_in_dim(live_mask, which * block, block, 0)
        emb_add, deg_add = block_terms(land_blk, fac_blk, mask_blk)
        return (sums[0] + emb_add, sums[1] + deg_add)

    emb_sum, deg_sum = lax.fori_loop(0, columns // block, turn, (emb_sum, deg_sum))
    raw_sum, degree, live = (emb_sum, deg_sum, live)
    scaled = raw_sum * lax.rsqrt(degree)
    squares = lax.psum(jnp.sum(scaled * scaled, axis=1, keepdims=True), ("grp", "blk"))
    total_pixels = pix_cols * lax.axis_size("grp") * lax.axis_size("blk")
    norms = jnp.sqrt(squares / total_pixels + 1e-06)
    return (scaled / norms, jnp.log(degree / live))


def solution(mesh):
    placed = (
        P(None, ("grp", "blk")),
        P(None, ("grp", "blk")),
        P(None, ("grp", "blk")),
        P(None, ("grp", "blk")),
    )
    return jax.shard_map(
        per_device,
        mesh=mesh,
        in_specs=placed,
        out_specs=(P(None, ("grp", "blk")), P(None, ("grp", "blk"))),
        check_vma=False,
    )
```

profile of v0, /device:TPU:0, one launch (start us, length us, event | category | flops | bytes accessed | tf_op | source)
XLA Modules:
  0.0 253.7 jit_solution(4222329401859136528)
XLA Ops:
  1.3 0.7 fusion.11
  1.9 0.7 compare_and_fusion
  2.6 42.0 %all-reduce = s32[32]{0:T(128)S(1)} all-reduce(s32[32]{0:T(128)S(1)} %bitcast_dynamic-update-slice_fusion), channel_id=1, replica_groups=mesh['grp'=8,'blk'=4] {'grp','blk'}, use_global_device_ids=true, to_apply=%add | all-reduce | flops 32 | bytes 256
  44.7 0.6 convert_reduce_fusion.1
  45.3 0.9 multiply_reduce_fusion.2
  46.3 70.7 %all_gather.9 = bf16[64,4096]{1,0:T(8,128)(2,1)S(1)} all-gather(bf16[64,128]{1,0:T(8,128)(2,1)} %param.9), channel_id=1, replica_groups=mesh['grp'=8,'blk'=4] {'grp','blk'}, dimensions={1}, use_global_device_ids=true | all-gather | bytes 540672 | tf_op jit(solution)/shard_map/all_gather | solution.py:29
  117.0 1.2 copy.6
  118.2 0.7 gather_fusion
  119.0 73.7 %all_gather.11 = bf16[32,4096]{0,1:T(8,128)(2,1)S(1)} all-gather(bf16[32,128]{0,1:T(8,128)(2,1)S(1)} %select_bitcast_fusion), channel_id=1, replica_groups=mesh['grp'=8,'blk'=4] {'grp','blk'}, dimensions={1}, use_global_device_ids=true | all-gather | bytes 270336 | tf_op jit(solution)/shard_map/all_gather | solution.py:28
  193.1 20.2 %while.16 = (s32[]{:T(128)}, f32[64,2048]{1,0:T(8,128)S(1)}, f32[1,2048]{1,0:T(1,128)S(1)}, bf16[64,4096]{1,0:T(8,128)(2,1)S(1)}, pred[4096,1]{0,1:T(4,128)(4,1)...) while((s32[]{:T(128)}, f32[64,2048]{1,0:T(8,128)S(1)}, ...), condition=%wide.region_4.5_spmd.clone, body=%wide.region_1.0_spmd.clone.sunk | while | flops 105146112 | bytes 3386566 | solution.py:44
  193.1 0.8 convert_reduce_fusion.3
  194.4 0.8 convert_reduce_fusion.3
  195.7 0.8 convert_reduce_fusion.3
  196.5 0.3 convolution_add_fusion.2
  196.9 0.8 convert_reduce_fusion.3
  198.2 0.8 convert_reduce_fusion.3
  199.5 0.8 convert_reduce_fusion.3
  200.7 0.8 convert_reduce_fusion.3
  201.6 0.3 convolution_add_fusion.2
  202.0 0.8 convert_reduce_fusion.3
  203.3 0.8 convert_reduce_fusion.3
  204.5 0.8 convert_reduce_fusion.3
  205.8 0.8 convert_reduce_fusion.3
  206.6 0.3 convolution_add_fusion.2
  207.1 0.8 convert_reduce_fusion.3
  208.3 0.8 convert_reduce_fusion.3
  209.6 0.8 convert_reduce_fusion.3
  210.9 0.8 convert_reduce_fusion.3
  212.1 0.8 convert_reduce_fusion.3
  213.3 1.3 divide_log_fusion
  214.8 38.0 %psum.7 = f32[64,1]{0,1:T(1,128)S(1)} all-reduce(f32[64,1]{0,1:T(1,128)S(1)} %bitcast.40), channel_id=1, replica_groups=mesh['grp'=8,'blk'=4] {'grp','blk'}, use_global_device_ids=true, to_apply=%region_6.7 | all-reduce | flops 64 | bytes 512 | tf_op jit(solution)/shard_map/psum | solution.py:47
  252.8 0.9 multiply_divide_fusion
  (74 shorter events, 6.2 us)
Async XLA Ops:
  119.0 74.1 %copy-start = (bf16[32,2048]{1,0:T(8,128)(2,1)S(1)}, bf16[32,2048]{1,0:T(8,128)(2,1)}, u32[]{:S(2)}) copy-start(bf16[32,2048]{1,0:T(8,128)(2,1)} %param.6) | copy-start | bytes 393220
where the time goes:
time: 254 us
  blocking collectives  224 us (88%)
  matrix products  18.4 us (7%)
  other arithmetic  6.17 us (2%)
  local copies, waits for them, and re-layouts  2.67 us (1%)
    all_gather x1, blocking collectives, per_device(): land_part = lax.all_gather(land, ('grp', 'blk'), axis=1, tiled=True)  73.7 us
    all_gather x1, blocking collectives, per_device(): fac_part = lax.all_gather(factor, ('grp', 'blk'), axis=1, tiled=True)  70.7 us
    unnamed x1, blocking collectives  42 us
    psum x1, blocking collectives, per_device(): lax.psum(jnp.sum(scaled * scaled, axis=1, keepdims=True), ('grp', 'blk'))  38 us
    dot_general x16, matrix products, block_terms(): lax.dot_general(land_blk, pixels, (((0,), (0,)), ((), ())), preferred_ele...  13.1 us
    dot_general x16, matrix products, block_terms(): emb_add = jnp.dot(fac_blk, kern, preferred_element_type=jnp.float32)  5.26 us

commit v1 on v0

v1 whole, which is shorter than its diff:
```python
import functools

import jax
import jax.numpy as jnp
from jax import lax
from jax.experimental import pallas as pl
from jax.experimental.pallas import tpu as pltpu
from jax.sharding import PartitionSpec as P

MESH = pl.DeviceIdType.MESH
AUX = 16
CHUNK = 512


def three_way(value):
    high = value.astype(jnp.bfloat16)
    rest = value - high.astype(jnp.float32)
    mid = rest.astype(jnp.bfloat16)
    low = (rest - mid.astype(jnp.float32)).astype(jnp.bfloat16)
    return [part.astype(jnp.float32) for part in (high, mid, low)]


def kernel(
    groups, depth, counts_ref, index_ref, pixels_ref, factor_ref,
    scaled_ref, inv_ref, logdeg_ref,
    blocks, pix_aug, acc, rows_a, rows_b,
    recv_sem, z_sem, chip_sem, sib_sem, ra_send, ra_recv, rb_send, rb_recv,
):
    layers, pix = pixels_ref.shape
    emb, cap = factor_ref.shape
    chips = groups // 2
    g, z = lax.axis_index("grp"), lax.axis_index("blk")
    core, chip = lax.rem(g, 2), lax.div(g, 2)
    sib = g + 1 - 2 * core

    barrier = pltpu.get_barrier_semaphore()

    def greet_group(k, carry):
        pl.semaphore_signal(
            barrier, inc=1, device_id=(lax.rem(g + k, groups), z), device_id_type=MESH
        )
        return carry

    def greet_depth(k, carry):
        pl.semaphore_signal(
            barrier, inc=1, device_id=(g, lax.rem(z + k, depth)), device_id_type=MESH
        )
        return carry

    lax.fori_loop(1, groups, greet_group, 0)
    lax.fori_loop(1, depth, greet_depth, 0)

    pick = lax.broadcasted_iota(jnp.int32, (pix, cap), 0) == index_ref[...]
    land = jnp.dot(
        pixels_ref[...], pick.astype(jnp.bfloat16), preferred_element_type=jnp.float32
    )
    alive = lax.broadcasted_iota(jnp.int32, (1, cap), 1) < counts_ref[0, 0]
    land_sq = jnp.where(alive, jnp.sum(land * land, axis=0, keepdims=True) * (-0.0625), -1e30)
    row = lax.broadcasted_iota(jnp.int32, (AUX, cap), 0)
    aux = jnp.where(row < 3, 1.0, 0.0)
    for at, part in enumerate(three_way(land_sq)):
        aux = jnp.where(row == 3 + at, part, aux)
    mine = blocks.at[chip * depth + z, core]
    mine[0:emb, :] = factor_ref[...]
    mine[emb : emb + AUX, :] = aux.astype(jnp.bfloat16)
    mine[emb + AUX : emb + AUX + layers, :] = land.astype(jnp.bfloat16)

    pl.semaphore_wait(barrier, groups + depth - 2)

    def send(slot, which, device, send_sem):
        ref = blocks.at[slot, which]
        return pltpu.make_async_remote_copy(
            src_ref=ref, dst_ref=ref, send_sem=send_sem, recv_sem=recv_sem.at[slot, which],
            device_id=device, device_id_type=MESH,
        )

    def slot_of(dc, dz):
        return lax.rem(chip + dc, chips) * depth + lax.rem(z + dz, depth)

    def to_depth(dz):
        return send(slot_of(0, 0), core, (g, lax.rem(z + dz, depth)), z_sem.at[dz])

    def to_chip(dz, dc):
        there = lax.rem(chip + dc, chips) * 2 + core
        return send(slot_of(0, dz), core, (there, z), chip_sem.at[dz, dc])

    def to_sib(dc, dz):
        return send(slot_of(dc, dz), core, (sib, z), sib_sem.at[dc, dz])

    def arrived(slot, which):
        send(slot, which, (sib, z), sib_sem.at[0, 0]).wait_recv()

    to_sib(0, 0).start()
    for dz in range(1, depth):
        to_depth(dz).start()
    for dc in range(1, chips):
        to_chip(0, dc).start()

    for at in range(0, pix, CHUNK):
        cols = pl.ds(at, CHUNK)
        own = pixels_ref[:, cols].astype(jnp.float32)
        pix_sq = jnp.sum(own * own, axis=0, keepdims=True) * (-0.0625)
        prow = lax.broadcasted_iota(jnp.int32, (AUX, CHUNK), 0)
        side = jnp.where((prow >= 3) & (prow < 6), 1.0, 0.0)
        for put, part in enumerate(three_way(pix_sq)):
            side = jnp.where(prow == put, part, side)
        pix_aug[0:AUX, cols] = side.astype(jnp.bfloat16)
        pix_aug[AUX : AUX + layers, cols] = (own * 0.125).astype(jnp.bfloat16)
    acc[...] = jnp.zeros_like(acc)

    def absorb(slot):
        both = jnp.concatenate([blocks[slot, 0], blocks[slot, 1]], axis=1)
        fac = both[0 : emb + AUX]
        side = both[emb : emb + AUX + layers].astype(jnp.float32).T.astype(jnp.bfloat16)
        for at in range(0, pix, CHUNK):
            cols = pl.ds(at, CHUNK)
            expo = jnp.dot(side, pix_aug[:, cols], preferred_element_type=jnp.float32)
            kern = jnp.exp(expo).astype(jnp.bfloat16)
            acc[:, cols] += jnp.dot(fac, kern, preferred_element_type=jnp.float32)

    arrived(slot_of(0, 0), 1 - core)
    absorb(slot_of(0, 0))

    def relay(dz, carry):
        slot = slot_of(0, dz)
        arrived(slot, core)
        for dc in range(1, chips):
            to_chip(dz, dc).start()
        to_sib(0, dz).start()
        return carry

    lax.fori_loop(1, depth, relay, 0)

    def near(dc, carry):
        slot = slot_of(dc, 0)
        arrived(slot, core)
        to_sib(dc, 0).start()
        return carry

    lax.fori_loop(1, chips, near, 0)

    def column(dz, carry):
        slot = slot_of(0, dz)
        arrived(slot, 1 - core)
        absorb(slot)
        return carry

    lax.fori_loop(1, depth, column, 0)

    def rest(k, carry):
        dz, dc = lax.div(k, chips - 1), 1 + lax.rem(k, chips - 1)

        @pl.when(k + chips - 1 < depth * (chips - 1))
        def _():
            slot = slot_of(dc, dz + 1)
            arrived(slot, core)
            to_sib(dc, dz + 1).start()

        slot = slot_of(dc, dz)
        arrived(slot, 1 - core)
        absorb(slot)
        return carry

    lax.fori_loop(0, depth * (chips - 1), rest, 0)

    part = jnp.zeros((emb, 128), jnp.float32)
    for at in range(0, pix, 128):
        cols = pl.ds(at, 128)
        scaled = acc[0:emb, cols] * lax.rsqrt(acc[emb : emb + 1, cols])
        scaled_ref[:, cols] = scaled
        part = part + scaled * scaled
    tall = jnp.concatenate([part, jnp.zeros((128 - emb, 128), jnp.float32)], axis=0)
    total = jnp.sum(tall.T, axis=0, keepdims=True)
    lane = lax.broadcasted_iota(jnp.int32, (1, 128), 1)
    total = jnp.where(lane == emb, counts_ref[0, 0].astype(jnp.float32), total)

    def exchange(total, rows, count, device_of, send_sems, recv_sems):
        rows[0] = total

        def give(k):
            return pltpu.make_async_remote_copy(
                src_ref=rows.at[0], dst_ref=rows.at[k],
                send_sem=send_sems.at[k], recv_sem=recv_sems.at[k],
                device_id=device_of(k), device_id_type=MESH,
            )

        for k in range(1, count):
            give(k).start()
        for k in range(1, count):
            give(k).wait_recv()
            total = total + rows[k]
        for k in range(1, count):
            give(k).wait_send()
        return total

    total = exchange(total, rows_a, groups, lambda k: (lax.rem(g + k, groups), z), ra_send, ra_recv)
    total = exchange(total, rows_b, depth, lambda k: (g, lax.rem(z + k, depth)), rb_send, rb_recv)

    live = total[:, emb : emb + 1]
    logdeg_ref[...] = jnp.log(acc[emb : emb + 1, :] / live)
    inv = lax.rsqrt(total / (pix * groups * depth) + 1e-06)
    inv_ref[...] = jnp.broadcast_to(inv, (128, 128)).T[0:emb]

    for dz in range(1, depth):
        to_depth(dz).wait_send()
    for dz in range(depth):
        for dc in range(1, chips):
            to_chip(dz, dc).wait_send()
    for dc in range(chips):
        for dz in range(depth):
            to_sib(dc, dz).wait_send()


def per_device(groups, depth, pixels, landmark_index, counts, factor):
    layers, pix = pixels.shape
    emb, cap = factor.shape
    chips = groups // 2
    vmem = pl.BlockSpec(memory_space=pltpu.VMEM)
    dma = pltpu.SemaphoreType.DMA
    scaled, inv, logdeg = pl.pallas_call(
        functools.partial(kernel, groups, depth),
        out_shape=(
            jax.ShapeDtypeStruct((emb, pix), jnp.float32),
            jax.ShapeDtypeStruct((emb, 128), jnp.float32),
            jax.ShapeDtypeStruct((1, pix), jnp.float32),
        ),
        in_specs=[pl.BlockSpec(memory_space=pltpu.SMEM), vmem, vmem, vmem],
        out_specs=(vmem, vmem, vmem),
        scratch_shapes=[
            pltpu.VMEM((chips * depth, 2, emb + AUX + layers, cap), jnp.bfloat16),
            pltpu.VMEM((AUX + layers, pix), jnp.bfloat16),
            pltpu.VMEM((emb + AUX, pix), jnp.float32),
            pltpu.VMEM((groups, 1, 128), jnp.float32),
            pltpu.VMEM((depth, 1, 128), jnp.float32),
            dma((chips * depth, 2)),
            dma((depth,)),
            dma((depth, chips)),
            dma((chips, depth)),
            dma((groups,)),
            dma((groups,)),
            dma((depth,)),
            dma((depth,)),
        ],
        compiler_params=pltpu.CompilerParams(
            collective_id=0, has_side_effects=True, vmem_limit_bytes=40 * 1024 * 1024
        ),
        cost_estimate=pl.CostEstimate(
            flops=2 * pix * cap * groups * depth * (emb + layers),
            bytes_accessed=4 * emb * pix,
            transcendentals=pix * cap * groups * depth,
        ),
    )(counts, landmark_index, pixels, factor)
    return (scaled * inv[:, 0:1], logdeg)


def solution(mesh):
    placed = P(None, ("grp", "blk"))
    return jax.shard_map(
        functools.partial(per_device, mesh.shape["grp"], mesh.shape["blk"]),
        mesh=mesh,
        in_specs=(placed,) * 4,
        out_specs=(placed, placed),
        check_vma=False,
    )
```

time: 254 us -> 40 us (0.16)
  blocking collectives: 224 us -> 0 us
  Pallas kernels: 0 us -> 35.2 us
  matrix products: 18.4 us -> 0 us
  other arithmetic: 6.17 us -> 0.91 us
    all_gather x2 -> x0, blocking collectives: 144 us -> none  [the longest x1 73.7 us: per_device(): land_part = lax.all_gather(land, ('grp', 'blk'), axis=1, tiled=True)]
    unnamed x1 -> x0, blocking collectives: 42 us -> none
    psum x1 -> x0, blocking collectives: 38 us -> none  [per_device(): lax.psum(jnp.sum(scaled * scaled, axis=1, keepdims=True), ('grp', 'blk'))]
    pallas_call x0 -> x1, Pallas kernels: none -> 35.2 us  [per_device(): pl.pallas_call(functools.partial(kernel, groups, depth), out_shape=(jax.S...]
    dot_general x32 -> x0, matrix products: 18.4 us -> none  [the longest x16 13.1 us: block_terms(): lax.dot_general(land_blk, pixels, (((0,), (0,)), ((), ())), preferred_ele...]
where the time goes in v1:
time: 40 us; the launch traced here: 39.8 us
  Pallas kernels  35.2 us (88%)
  local copies, waits for them, and re-layouts  2.32 us (6%)
  between operations  1.33 us (3%)
  other arithmetic  0.91 us (2%)
    pallas_call x1, Pallas kernels, per_device(): pl.pallas_call(functools.partial(kernel, groups, depth), out_shape=(jax.S...  35.2 us
    unnamed x7, local copies, waits for them, and re-layouts  2.22 us
    mul x1, other arithmetic, per_device(): return (scaled * inv[:, 0:1], logdeg)  0.91 us

profile of v1, /device:TPU:0, one launch (start us, length us, event | category | flops | bytes accessed | tf_op | source)
XLA Modules:
  0.0 39.8 jit_solution(1642058206595437530)
XLA Ops:
  0.6 0.0 copy-start.2
  1.3 0.0 copy-done.2
  1.3 0.0 copy-start
  1.3 0.9 %copy-done = bf16[32,2048]{1,0:T(8,128)(2,1)S(1)} copy-done((bf16[32,2048]{1,0:T(8,128)(2,1)S(1)}, bf16[32,2048]{1,0:T(8,128)(2,1)}, u32[]{:S(2)}) %copy-start) | copy-done | bytes 131096
  2.2 0.0 copy-start.1
  2.2 0.7 %copy-done.1 = bf16[64,128]{1,0:T(8,128)(2,1)S(1)} copy-done((bf16[64,128]{1,0:T(8,128)(2,1)S(1)}, bf16[64,128]{1,0:T(8,128)(2,1)}, u32[]{:S(2)}) %copy-start.1) | copy-done | bytes 16408
  2.9 35.2 %shard_map.59 = (f32[64,2048]{1,0:T(8,128)S(1)}, f32[64,128]{1,0:T(8,128)S(1)}, f32[1,2048]{1,0:T(1,128)S(1)}) custom-call(s32[1,1]{1,0:T(1,128)S(6)} %copy.7.counts_ref, s32[1,128]{1,0:T(1,128)S(1)} %copy-done.2, bf16[32,2048]{1,0:T(8,128)(2,1)S(1)} %copy-done, bf16[64,128]{1,0:T(8,128)(2,1)S(1)} %copy-done.1), custom_call_target="tpu_custom_call" | custom-call | flops 1610612736 | bytes 524288 | tf_op jit(solution)/shard_map/pallas_call | solution.py:220
  38.1 0.1 slice_reduce_fusion
  38.2 0.9 %broadcast_multiply_fusion = f32[64,2048]{1,0:T(8,128)} fusion(f32[64,2048]{1,0:T(8,128)S(1)} %get-tuple-element.5, f32[64]{0:T(128)S(1)} %slice_reduce_fusion), kind=kLoop, calls=%fused_computation | loop fusion | flops 131072 | bytes 1048832 | tf_op jit(solution)/shard_map/mul | solution.py:253
  39.2 0.6 %copy.8 = f32[1,2048]{1,0:T(1,128)} copy(f32[1,2048]{1,0:T(1,128)S(1)} %get-tuple-element.11) | data formatting | bytes 16384
Async XLA Ops:
  0.6 0.7 %copy-start.2 = (s32[1,128]{1,0:T(1,128)S(1)}, s32[1,128]{1,0:T(1,128)}, u32[]{:S(2)}) copy-start(s32[1,128]{1,0:T(1,128)} %index_ref.1) | copy-start | bytes 1540
  1.3 0.9 %copy-start = (bf16[32,2048]{1,0:T(8,128)(2,1)S(1)}, bf16[32,2048]{1,0:T(8,128)(2,1)}, u32[]{:S(2)}) copy-start(bf16[32,2048]{1,0:T(8,128)(2,1)} %pixels_ref.1) | copy-start | bytes 393220
  2.2 0.7 %copy-start.1 = (bf16[64,128]{1,0:T(8,128)(2,1)S(1)}, bf16[64,128]{1,0:T(8,128)(2,1)}, u32[]{:S(2)}) copy-start(bf16[64,128]{1,0:T(8,128)(2,1)} %factor_ref.1) | copy-start | bytes 49156

commit v2 on v1

--- a/solution.py
+++ b/solution.py
@@ -9,7 +9,9 @@
 
 MESH = pl.DeviceIdType.MESH
 AUX = 16
-CHUNK = 512
+CHUNK = 256
+TOGETHER = 3
+OUT = 512
 
 
 def three_way(value):
@@ -21,17 +23,33 @@
 
 
 def kernel(
-    groups, depth, counts_ref, index_ref, pixels_ref, factor_ref,
+    groups, depth, pixels_in, index_in, counts_in, factor_in,
     scaled_ref, inv_ref, logdeg_ref,
+    pixels_ref, index_ref, counts_ref, in_sem,
     blocks, pix_aug, acc, rows_a, rows_b,
     recv_sem, z_sem, chip_sem, sib_sem, ra_send, ra_recv, rb_send, rb_recv,
 ):
-    layers, pix = pixels_ref.shape
-    emb, cap = factor_ref.shape
+    layers, pix = pixels_in.shape
+    emb, cap = factor_in.shape
     chips = groups // 2
     g, z = lax.axis_index("grp"), lax.axis_index("blk")
     core, chip = lax.rem(g, 2), lax.div(g, 2)
     sib = g + 1 - 2 * core
+    mine = blocks.at[chip * depth + z, core]
+
+    loads = [
+        pltpu.make_async_copy(src, dst, in_sem.at[at])
+        for at, (src, dst) in enumerate(
+            [
+                (pixels_in, pixels_ref),
+                (index_in, index_ref),
+                (counts_in, counts_ref),
+                (factor_in, mine.at[0:emb, :]),
+            ]
+        )
+    ]
+    for load in loads:
+        load.start()
 
     barrier = pltpu.get_barrier_semaphore()
 
@@ -49,19 +67,20 @@
 
     lax.fori_loop(1, groups, greet_group, 0)
     lax.fori_loop(1, depth, greet_depth, 0)
+
+    for load in loads:
+        load.wait()
 
     pick = lax.broadcasted_iota(jnp.int32, (pix, cap), 0) == index_ref[...]
     land = jnp.dot(
         pixels_ref[...], pick.astype(jnp.bfloat16), preferred_element_type=jnp.float32
     )
-    alive = lax.broadcasted_iota(jnp.int32, (1, cap), 1) < counts_ref[0, 0]
+    alive = lax.broadcasted_iota(jnp.int32, (1, cap), 1) < counts_ref[...]
     land_sq = jnp.where(alive, jnp.sum(land * land, axis=0, keepdims=True) * (-0.0625), -1e30)
     row = lax.broadcasted_iota(jnp.int32, (AUX, cap), 0)
     aux = jnp.where(row < 3, 1.0, 0.0)
     for at, part in enumerate(three_way(land_sq)):
         aux = jnp.where(row == 3 + at, part, aux)
-    mine = blocks.at[chip * depth + z, core]
-    mine[0:emb, :] = factor_ref[...]
     mine[emb : emb + AUX, :] = aux.astype(jnp.bfloat16)
     mine[emb + AUX : emb + AUX + layers, :] = land.astype(jnp.bfloat16)
 
@@ -108,15 +127,26 @@
         pix_aug[AUX : AUX + layers, cols] = (own * 0.125).astype(jnp.bfloat16)
     acc[...] = jnp.zeros_like(acc)
 
-    def absorb(slot):
-        both = jnp.concatenate([blocks[slot, 0], blocks[slot, 1]], axis=1)
-        fac = both[0 : emb + AUX]
-        side = both[emb : emb + AUX + layers].astype(jnp.float32).T.astype(jnp.bfloat16)
+    def absorb(*slots):
+        fac = jnp.concatenate(
+            [blocks[slot, half, 0 : emb + AUX] for slot in slots for half in range(2)], axis=1
+        )
+        side = jnp.concatenate(
+            [
+                blocks[slot, half, emb : emb + AUX + layers].astype(jnp.float32).T
+                for slot in slots
+                for half in range(2)
+            ],
+            axis=0,
+        ).astype(jnp.bfloat16)
         for at in range(0, pix, CHUNK):
             cols = pl.ds(at, CHUNK)
             expo = jnp.dot(side, pix_aug[:, cols], preferred_element_type=jnp.float32)
             kern = jnp.exp(expo).astype(jnp.bfloat16)
             acc[:, cols] += jnp.dot(fac, kern, preferred_element_type=jnp.float32)
+
+    def bunches(count):
+        return [range(at, min(at + TOGETHER, count)) for at in range(1, count, TOGETHER)]
 
     arrived(slot_of(0, 0), 1 - core)
     absorb(slot_of(0, 0))
@@ -139,29 +169,25 @@
 
     lax.fori_loop(1, chips, near, 0)
 
-    def column(dz, carry):
-        slot = slot_of(0, dz)
-        arrived(slot, 1 - core)
-        absorb(slot)
-        return carry
-
-    lax.fori_loop(1, depth, column, 0)
-
-    def rest(k, carry):
-        dz, dc = lax.div(k, chips - 1), 1 + lax.rem(k, chips - 1)
-
-        @pl.when(k + chips - 1 < depth * (chips - 1))
+    for bunch in bunches(depth):
+        for dz in bunch:
+            arrived(slot_of(0, dz), 1 - core)
+        absorb(*[slot_of(0, dz) for dz in bunch])
+
+    def rest(dz, carry):
+        @pl.when(dz + 1 < depth)
         def _():
-            slot = slot_of(dc, dz + 1)
-            arrived(slot, core)
-            to_sib(dc, dz + 1).start()
-
-        slot = slot_of(dc, dz)
-        arrived(slot, 1 - core)
-        absorb(slot)
-        return carry
-
-    lax.fori_loop(0, depth * (chips - 1), rest, 0)
+            for dc in range(1, chips):
+                arrived(slot_of(dc, dz + 1), core)
+                to_sib(dc, dz + 1).start()
+
+        for bunch in bunches(chips):
+            for dc in bunch:
+                arrived(slot_of(dc, dz), 1 - core)
+            absorb(*[slot_of(dc, dz) for dc in bunch])
+        return carry
+
+    lax.fori_loop(0, depth, rest, 0)
 
     part = jnp.zeros((emb, 128), jnp.float32)
     for at in range(0, pix, 128):
@@ -172,7 +198,7 @@
     tall = jnp.concatenate([part, jnp.zeros((128 - emb, 128), jnp.float32)], axis=0)
     total = jnp.sum(tall.T, axis=0, keepdims=True)
     lane = lax.broadcasted_iota(jnp.int32, (1, 128), 1)
-    total = jnp.where(lane == emb, counts_ref[0, 0].astype(jnp.float32), total)
+    total = jnp.where(lane == emb, counts_ref[...].astype(jnp.float32), total)
 
     def exchange(total, rows, count, device_of, send_sems, recv_sems):
         rows[0] = total
@@ -209,6 +235,23 @@
     for dc in range(chips):
         for dz in range(depth):
             to_sib(dc, dz).wait_send()
+
+
+def finish(scaled_ref, inv_ref, logdeg_ref, emb_out, logdeg_out, held, sems):
+    pix = scaled_ref.shape[1]
+    copies = [pltpu.make_async_copy(logdeg_ref, logdeg_out, sems.at[pix // OUT])]
+    copies[0].start()
+    inv = inv_ref[...]
+    for step in range(pix // OUT):
+        for at in range(step * OUT, (step + 1) * OUT, 128):
+            cols = pl.ds(at, 128)
+            held[:, cols] = scaled_ref[:, cols] * inv
+        cols = pl.ds(step * OUT, OUT)
+        copy = pltpu.make_async_copy(held.at[:, cols], emb_out.at[:, cols], sems.at[step])
+        copy.start()
+        copies.append(copy)
+    for copy in copies:
+        copy.wait()
 
 
 def per_device(groups, depth, pixels, landmark_index, counts, factor):
@@ -224,9 +267,13 @@
             jax.ShapeDtypeStruct((emb, 128), jnp.float32),
             jax.ShapeDtypeStruct((1, pix), jnp.float32),
         ),
-        in_specs=[pl.BlockSpec(memory_space=pltpu.SMEM), vmem, vmem, vmem],
+        in_specs=[pl.BlockSpec(memory_space=pltpu.HBM)] * 4,
         out_specs=(vmem, vmem, vmem),
         scratch_shapes=[
+            pltpu.VMEM((layers, pix), jnp.bfloat16),
+            pltpu.VMEM((1, cap), jnp.int32),
+            pltpu.VMEM((1, 1), jnp.int32),
+            dma((4,)),
             pltpu.VMEM((chips * depth, 2, emb + AUX + layers, cap), jnp.bfloat16),
             pltpu.VMEM((AUX + layers, pix), jnp.bfloat16),
             pltpu.VMEM((emb + AUX, pix), jnp.float32),
@@ -249,8 +296,21 @@
             bytes_accessed=4 * emb * pix,
             transcendentals=pix * cap * groups * depth,
         ),
-    )(counts, landmark_index, pixels, factor)
-    return (scaled * inv[:, 0:1], logdeg)
+    )(pixels, landmark_index, counts, factor)
+    anywhere = pl.BlockSpec(memory_space=pltpu.HBM)
+    return pl.pallas_call(
+        finish,
+        out_shape=(
+            jax.ShapeDtypeStruct((emb, pix), jnp.float32),
+            jax.ShapeDtypeStruct((1, pix), jnp.float32),
+        ),
+        in_specs=[vmem, vmem, vmem],
+        out_specs=(anywhere, anywhere),
+        scratch_shapes=[pltpu.VMEM((emb, pix), jnp.float32), dma((pix // OUT + 1,))],
+        cost_estimate=pl.CostEstimate(
+            flops=emb * pix, bytes_accessed=8 * emb * pix, transcendentals=0
+        ),
+    )(scaled, inv, logdeg)
 
 
 def solution(mesh):

time: 40 us -> 41.2 us (1.030)
  local copies, waits for them, and re-layouts: 2.32 us -> 3.61 us
  other arithmetic: 0.91 us -> 0 us
  Pallas kernels: 35.2 us -> 36 us
    pallas_call x0 -> x1, Pallas kernels: none -> 1.9 us  [per_device(): pl.pallas_call(finish, out_shape=(jax.ShapeDtypeStruct((emb, pix), jnp.fl...]
    unnamed x7 -> x12, local copies, waits for them, and re-layouts: 2.22 us -> 3.61 us
    pallas_call x1, Pallas kernels: 35.2 us -> 34.1 us  [per_device(): pl.pallas_call(functools.partial(kernel, groups, depth), out_shape=(jax.S...]
    mul x1 -> x0, other arithmetic: 0.91 us -> none  [per_device(): return (scaled * inv[:, 0:1], logdeg)]
where the time goes in v2:
time: 41.2 us; the launch traced here: 41 us
  Pallas kernels  36 us (87%)
  local copies, waits for them, and re-layouts  3.61 us (9%)
  between operations  1.33 us (3%)
    pallas_call x1, Pallas kernels, per_device(): pl.pallas_call(functools.partial(kernel, groups, depth), out_shape=(jax.S...  34.1 us
    unnamed x12, local copies, waits for them, and re-layouts  3.61 us
    pallas_call x1, Pallas kernels, per_device(): pl.pallas_call(finish, out_shape=(jax.ShapeDtypeStruct((emb, pix), jnp.fl...  1.9 us

profile of v2, /device:TPU:0, one launch (start us, length us, event | category | flops | bytes accessed | tf_op | source)
XLA Modules:
  0.0 41.0 jit_solution(10485723867785664397)
XLA Ops:
  0.6 0.0 copy-start.5
  1.3 0.0 copy-done.5
  1.3 0.0 copy-start.3
  1.3 0.9 %copy-done.3 = bf16[32,2048]{1,0:T(8,128)(2,1)S(1)} copy-done((bf16[32,2048]{1,0:T(8,128)(2,1)S(1)}, bf16[32,2048]{1,0:T(8,128)(2,1)}, u32[]{:S(2)}) %copy-start.3) | copy-done | bytes 131096
  2.2 0.0 copy-start.4
  2.2 0.7 %copy-done.4 = bf16[64,128]{1,0:T(8,128)(2,1)S(1)} copy-done((bf16[64,128]{1,0:T(8,128)(2,1)S(1)}, bf16[64,128]{1,0:T(8,128)(2,1)}, u32[]{:S(2)}) %copy-start.4) | copy-done | bytes 16408
  2.9 34.1 %shard_map.59 = (f32[64,2048]{1,0:T(8,128)S(1)}, f32[64,128]{1,0:T(8,128)S(1)}, f32[1,2048]{1,0:T(1,128)S(1)}) custom-call(bf16[32,2048]{1,0:T(8,128)(2,1)S(1)} %copy-done.3, s32[1,128]{1,0:T(1,128)S(1)} %copy-done.5, s32[1,1]{1,0:T(1,128)S(6)} %copy.6.counts_in, bf16[64,128]{1,0:T(8,128)(2,1)S(1)} %copy-done.4), custom_call_target="tpu_custom_call" | custom-call | flops 1610612736 | bytes 524288 | tf_op jit(solution)/shard_map/pallas_call | solution.py:263
  37.1 0.0 copy-start
  37.1 0.8 %copy-done = f32[64,2048]{1,0:T(8,128)} copy-done((f32[64,2048]{1,0:T(8,128)}, f32[64,2048]{1,0:T(8,128)S(1)}, u32[]{:S(2)}) %copy-start) | copy-done | bytes 524312
  37.9 0.0 copy-start.1
  37.9 0.6 %copy-done.1 = f32[64,128]{1,0:T(8,128)} copy-done((f32[64,128]{1,0:T(8,128)}, f32[64,128]{1,0:T(8,128)S(1)}, u32[]{:S(2)}) %copy-start.1) | copy-done | bytes 32792
  38.5 0.0 copy-start.2
  38.5 0.6 %copy-done.2 = f32[1,2048]{1,0:T(1,128)} copy-done((f32[1,2048]{1,0:T(1,128)}, f32[1,2048]{1,0:T(1,128)S(1)}, u32[]{:S(2)}) %copy-start.2) | copy-done | bytes 8216
  39.1 1.9 %shard_map.60 = (f32[64,2048]{1,0:T(8,128)}, f32[1,2048]{1,0:T(1,128)}) custom-call(f32[64,2048]{1,0:T(8,128)} %copy-done, f32[64,128]{1,0:T(8,128)} %copy-done.1, f32[1,2048]{1,0:T(1,128)} %copy-done.2), custom_call_target="tpu_custom_call" | custom-call | flops 131072 | bytes 1048576 | tf_op jit(solution)/shard_map/pallas_call | solution.py:301
Async XLA Ops:
  0.6 0.7 %copy-start.5 = (s32[1,128]{1,0:T(1,128)S(1)}, s32[1,128]{1,0:T(1,128)}, u32[]{:S(2)}) copy-start(s32[1,128]{1,0:T(1,128)} %index_in.1) | copy-start | bytes 1540
  1.3 0.9 %copy-start.3 = (bf16[32,2048]{1,0:T(8,128)(2,1)S(1)}, bf16[32,2048]{1,0:T(8,128)(2,1)}, u32[]{:S(2)}) copy-start(bf16[32,2048]{1,0:T(8,128)(2,1)} %pixels_in.1) | copy-start | bytes 393220
  2.2 0.7 %copy-start.4 = (bf16[64,128]{1,0:T(8,128)(2,1)S(1)}, bf16[64,128]{1,0:T(8,128)(2,1)}, u32[]{:S(2)}) copy-start(bf16[64,128]{1,0:T(8,128)(2,1)} %factor_in.1) | copy-start | bytes 49156
  37.1 0.8 %copy-start = (f32[64,2048]{1,0:T(8,128)}, f32[64,2048]{1,0:T(8,128)S(1)}, u32[]{:S(2)}) copy-start(f32[64,2048]{1,0:T(8,128)S(1)} %get-tuple-element.5.scaled_ref) | copy-start | bytes 1572868
  37.9 0.6 %copy-start.1 = (f32[64,128]{1,0:T(8,128)}, f32[64,128]{1,0:T(8,128)S(1)}, u32[]{:S(2)}) copy-start(f32[64,128]{1,0:T(8,128)S(1)} %get-tuple-element.6.inv_ref) | copy-start | bytes 98308
  38.5 0.6 %copy-start.2 = (f32[1,2048]{1,0:T(1,128)}, f32[1,2048]{1,0:T(1,128)S(1)}, u32[]{:S(2)}) copy-start(f32[1,2048]{1,0:T(1,128)S(1)} %get-tuple-element.7.logdeg_ref) | copy-start | bytes 24580

commit v3 on v2

--- a/solution.py
+++ b/solution.py
@@ -11,7 +11,6 @@
 AUX = 16
 CHUNK = 256
 TOGETHER = 3
-OUT = 512
 
 
 def three_way(value):
@@ -25,7 +24,7 @@
 def kernel(
     groups, depth, pixels_in, index_in, counts_in, factor_in,
     scaled_ref, inv_ref, logdeg_ref,
-    pixels_ref, index_ref, counts_ref, in_sem,
+    pixels_ref, index_ref, counts_ref, in_sem, out_sem,
     blocks, pix_aug, acc, rows_a, rows_b,
     recv_sem, z_sem, chip_sem, sib_sem, ra_send, ra_recv, rb_send, rb_recv,
 ):
@@ -139,11 +138,19 @@
             ],
             axis=0,
         ).astype(jnp.bfloat16)
+
+        def exponent(at):
+            return jnp.dot(
+                side, pix_aug[:, at : at + CHUNK], preferred_element_type=jnp.float32
+            )
+
+        ahead = exponent(0)
         for at in range(0, pix, CHUNK):
-            cols = pl.ds(at, CHUNK)
-            expo = jnp.dot(side, pix_aug[:, cols], preferred_element_type=jnp.float32)
+            expo = ahead
+            if at + CHUNK < pix:
+                ahead = exponent(at + CHUNK)
             kern = jnp.exp(expo).astype(jnp.bfloat16)
-            acc[:, cols] += jnp.dot(fac, kern, preferred_element_type=jnp.float32)
+            acc[:, at : at + CHUNK] += jnp.dot(fac, kern, preferred_element_type=jnp.float32)
 
     def bunches(count):
         return [range(at, min(at + TOGETHER, count)) for at in range(1, count, TOGETHER)]
@@ -193,8 +200,10 @@
     for at in range(0, pix, 128):
         cols = pl.ds(at, 128)
         scaled = acc[0:emb, cols] * lax.rsqrt(acc[emb : emb + 1, cols])
-        scaled_ref[:, cols] = scaled
+        acc[0:emb, cols] = scaled
         part = part + scaled * scaled
+    give_scaled = pltpu.make_async_copy(acc.at[0:emb, :], scaled_ref, out_sem)
+    give_scaled.start()
     tall = jnp.concatenate([part, jnp.zeros((128 - emb, 128), jnp.float32)], axis=0)
     total = jnp.sum(tall.T, axis=0, keepdims=True)
     lane = lax.broadcasted_iota(jnp.int32, (1, 128), 1)
@@ -227,6 +236,7 @@
     inv = lax.rsqrt(total / (pix * groups * depth) + 1e-06)
     inv_ref[...] = jnp.broadcast_to(inv, (128, 128)).T[0:emb]
 
+    give_scaled.wait()
     for dz in range(1, depth):
         to_depth(dz).wait_send()
     for dz in range(depth):
@@ -235,23 +245,6 @@
     for dc in range(chips):
         for dz in range(depth):
             to_sib(dc, dz).wait_send()
-
-
-def finish(scaled_ref, inv_ref, logdeg_ref, emb_out, logdeg_out, held, sems):
-    pix = scaled_ref.shape[1]
-    copies = [pltpu.make_async_copy(logdeg_ref, logdeg_out, sems.at[pix // OUT])]
-    copies[0].start()
-    inv = inv_ref[...]
-    for step in range(pix // OUT):
-        for at in range(step * OUT, (step + 1) * OUT, 128):
-            cols = pl.ds(at, 128)
-            held[:, cols] = scaled_ref[:, cols] * inv
-        cols = pl.ds(step * OUT, OUT)
-        copy = pltpu.make_async_copy(held.at[:, cols], emb_out.at[:, cols], sems.at[step])
-        copy.start()
-        copies.append(copy)
-    for copy in copies:
-        copy.wait()
 
 
 def per_device(groups, depth, pixels, landmark_index, counts, factor):
@@ -268,12 +261,13 @@
             jax.ShapeDtypeStruct((1, pix), jnp.float32),
         ),
         in_specs=[pl.BlockSpec(memory_space=pltpu.HBM)] * 4,
-        out_specs=(vmem, vmem, vmem),
+        out_specs=(pl.BlockSpec(memory_space=pltpu.HBM), vmem, vmem),
         scratch_shapes=[
             pltpu.VMEM((layers, pix), jnp.bfloat16),
             pltpu.VMEM((1, cap), jnp.int32),
             pltpu.VMEM((1, 1), jnp.int32),
             dma((4,)),
+            dma,
             pltpu.VMEM((chips * depth, 2, emb + AUX + layers, cap), jnp.bfloat16),
             pltpu.VMEM((AUX + layers, pix), jnp.bfloat16),
             pltpu.VMEM((emb + AUX, pix), jnp.float32),
@@ -289,7 +283,7 @@
             dma((depth,)),
         ],
         compiler_params=pltpu.CompilerParams(
-            collective_id=0, has_side_effects=True, vmem_limit_bytes=40 * 1024 * 1024
+            collective_id=0, has_side_effects=True, vmem_limit_bytes=56 * 1024 * 1024
         ),
         cost_estimate=pl.CostEstimate(
             flops=2 * pix * cap * groups * depth * (emb + layers),
@@ -297,20 +291,7 @@
             transcendentals=pix * cap * groups * depth,
         ),
     )(pixels, landmark_index, counts, factor)
-    anywhere = pl.BlockSpec(memory_space=pltpu.HBM)
-    return pl.pallas_call(
-        finish,
-        out_shape=(
-            jax.ShapeDtypeStruct((emb, pix), jnp.float32),
-            jax.ShapeDtypeStruct((1, pix), jnp.float32),
-        ),
-        in_specs=[vmem, vmem, vmem],
-        out_specs=(anywhere, anywhere),
-        scratch_shapes=[pltpu.VMEM((emb, pix), jnp.float32), dma((pix // OUT + 1,))],
-        cost_estimate=pl.CostEstimate(
-            flops=emb * pix, bytes_accessed=8 * emb * pix, transcendentals=0
-        ),
-    )(scaled, inv, logdeg)
+    return (scaled * inv[:, 0:1], logdeg)
 
 
 def solution(mesh):

time: 41.2 us -> 33.6 us (0.82)
  Pallas kernels: 36 us -> 28.7 us
  local copies, waits for them, and re-layouts: 3.61 us -> 1.47 us
  other arithmetic: 0 us -> 1.95 us
    pallas_call x1, Pallas kernels: 34.1 us -> 28.7 us  [per_device(): pl.pallas_call(functools.partial(kernel, groups, depth), out_shape=(jax.S...]
    unnamed x12 -> x3, local copies, waits for them, and re-layouts: 3.61 us -> 0.6 us
    mul x0 -> x1, other arithmetic: none -> 1.95 us  [per_device(): return (scaled * inv[:, 0:1], logdeg)]
    pallas_call x1 -> x0, Pallas kernels: 1.9 us -> none  [per_device(): pl.pallas_call(finish, out_shape=(jax.ShapeDtypeStruct((emb, pix), jnp.fl...]
    slice x0 -> x1, local copies, waits for them, and re-layouts: none -> 0.86 us  [per_device(): return (scaled * inv[:, 0:1], logdeg)]
where the time goes in v3:
time: 33.6 us; the launch traced here: 33.4 us
  Pallas kernels  28.7 us (85%)
  other arithmetic  1.95 us (6%)
  local copies, waits for them, and re-layouts  1.47 us (4%)
  between operations  1.3 us (4%)
    pallas_call x1, Pallas kernels, per_device(): pl.pallas_call(functools.partial(kernel, groups, depth), out_shape=(jax.S...  28.7 us
    mul x1, other arithmetic, per_device(): return (scaled * inv[:, 0:1], logdeg)  1.95 us
    slice x1, local copies, waits for them, and re-layouts, per_device(): return (scaled * inv[:, 0:1], logdeg)  0.86 us

profile of v3, /device:TPU:0, one launch (start us, length us, event | category | flops | bytes accessed | tf_op | source)
XLA Modules:
  0.0 33.4 jit_solution(12420217519604388201)
XLA Ops:
  1.3 28.7 %shard_map.59 = (f32[64,2048]{1,0:T(8,128)}, f32[64,128]{1,0:T(8,128)}, f32[1,2048]{1,0:T(1,128)}) custom-call(bf16[32,2048]{1,0:T(8,128)(2,1)} %pixels_in.1, s32[1,128]{1,0:T(1,128)} %index_in.1, s32[1,1]{1,0:T(1,128)S(6)} %copy.7.counts_in, bf16[64,128]{1,0:T(8,128)(2,1)} %factor_in.1), custom_call_target="tpu_custom_call" | custom-call | flops 1610612736 | bytes 524288 | tf_op jit(solution)/shard_map/pallas_call | solution.py:256
  30.0 0.9 %slice_reduce_fusion = f32[64]{0:T(128)S(1)} fusion(f32[64,128]{1,0:T(8,128)} %get-tuple-element.6), kind=kLoop, calls=%fused_computation.1 | loop fusion | bytes 512 | tf_op jit(solution)/shard_map/slice | solution.py:294
  30.9 0.0 copy-start
  30.9 2.0 %broadcast_multiply_fusion = f32[64,2048]{1,0:T(8,128)} fusion(f32[64,2048]{1,0:T(8,128)} %get-tuple-element.5, f32[64]{0:T(128)S(1)} %slice_reduce_fusion), kind=kLoop, calls=%fused_computation | loop fusion | flops 131072 | bytes 1048832 | tf_op jit(solution)/shard_map/mul | solution.py:294
  32.8 0.0 copy-done
  32.8 0.6 %copy.8 = f32[1,2048]{1,0:T(1,128)} copy(f32[1,2048]{1,0:T(1,128)S(1)} %copy-done) | data formatting | bytes 16384
Async XLA Ops:
  30.9 2.0 %copy-start = (f32[1,2048]{1,0:T(1,128)S(1)}, f32[1,2048]{1,0:T(1,128)}, u32[]{:S(2)}) copy-start(f32[1,2048]{1,0:T(1,128)} %get-tuple-element.11) | copy-start | bytes 24580

commit v4 on v3

--- a/solution.py
+++ b/solution.py
@@ -11,6 +11,7 @@
 AUX = 16
 CHUNK = 256
 TOGETHER = 3
+GIVE = 512
 
 
 def three_way(value):
@@ -23,7 +24,7 @@
 
 def kernel(
     groups, depth, pixels_in, index_in, counts_in, factor_in,
-    scaled_ref, inv_ref, logdeg_ref,
+    emb_ref, logdeg_ref,
     pixels_ref, index_ref, counts_ref, in_sem, out_sem,
     blocks, pix_aug, acc, rows_a, rows_b,
     recv_sem, z_sem, chip_sem, sib_sem, ra_send, ra_recv, rb_send, rb_recv,
@@ -127,30 +128,35 @@
     acc[...] = jnp.zeros_like(acc)
 
     def absorb(*slots):
-        fac = jnp.concatenate(
-            [blocks[slot, half, 0 : emb + AUX] for slot in slots for half in range(2)], axis=1
-        )
-        side = jnp.concatenate(
-            [
-                blocks[slot, half, emb : emb + AUX + layers].astype(jnp.float32).T
-                for slot in slots
-                for half in range(2)
-            ],
-            axis=0,
-        ).astype(jnp.bfloat16)
-
-        def exponent(at):
+        def both(slot, rows):
+            return [blocks[slot, half, rows] for half in range(2)]
+
+        facs = [jnp.concatenate(both(slot, slice(0, emb + AUX)), axis=1) for slot in slots]
+        sides = [
+            jnp.concatenate(
+                [half.astype(jnp.float32).T for half in both(slot, slice(emb, emb + AUX + layers))],
+                axis=0,
+            ).astype(jnp.bfloat16)
+            for slot in slots
+        ]
+        tiles = [(at, k) for at in range(0, pix, CHUNK) for k in range(len(slots))]
+
+        def exponent(at, k):
             return jnp.dot(
-                side, pix_aug[:, at : at + CHUNK], preferred_element_type=jnp.float32
+                sides[k], pix_aug[:, at : at + CHUNK], preferred_element_type=jnp.float32
             )
 
-        ahead = exponent(0)
-        for at in range(0, pix, CHUNK):
+        ahead = exponent(*tiles[0])
+        total = None
+        for turn, (at, k) in enumerate(tiles):
             expo = ahead
-            if at + CHUNK < pix:
-                ahead = exponent(at + CHUNK)
+            if turn + 1 < len(tiles):
+                ahead = exponent(*tiles[turn + 1])
             kern = jnp.exp(expo).astype(jnp.bfloat16)
-            acc[:, at : at + CHUNK] += jnp.dot(fac, kern, preferred_element_type=jnp.float32)
+            add = jnp.dot(facs[k], kern, preferred_element_type=jnp.float32)
+            total = add if k == 0 else total + add
+            if k + 1 == len(slots):
+                acc[:, at : at + CHUNK] += total
 
     def bunches(count):
         return [range(at, min(at + TOGETHER, count)) for at in range(1, count, TOGETHER)]
@@ -202,8 +208,6 @@
         scaled = acc[0:emb, cols] * lax.rsqrt(acc[emb : emb + 1, cols])
         acc[0:emb, cols] = scaled
         part = part + scaled * scaled
-    give_scaled = pltpu.make_async_copy(acc.at[0:emb, :], scaled_ref, out_sem)
-    give_scaled.start()
     tall = jnp.concatenate([part, jnp.zeros((128 - emb, 128), jnp.float32)], axis=0)
     total = jnp.sum(tall.T, axis=0, keepdims=True)
     lane = lax.broadcasted_iota(jnp.int32, (1, 128), 1)
@@ -231,12 +235,21 @@
     total = exchange(total, rows_a, groups, lambda k: (lax.rem(g + k, groups), z), ra_send, ra_recv)
     total = exchange(total, rows_b, depth, lambda k: (g, lax.rem(z + k, depth)), rb_send, rb_recv)
 
+    inv = lax.rsqrt(total / (pix * groups * depth) + 1e-06)
+    inv = jnp.broadcast_to(inv, (128, 128)).T[0:emb]
+    gives = []
+    for at in range(0, pix, GIVE):
+        for col in range(at, at + GIVE, 128):
+            acc[0:emb, col : col + 128] = acc[0:emb, col : col + 128] * inv
+        part = pl.ds(at, GIVE)
+        gives.append(
+            pltpu.make_async_copy(acc.at[0:emb, part], emb_ref.at[:, part], out_sem.at[at // GIVE])
+        )
+        gives[-1].start()
     live = total[:, emb : emb + 1]
     logdeg_ref[...] = jnp.log(acc[emb : emb + 1, :] / live)
-    inv = lax.rsqrt(total / (pix * groups * depth) + 1e-06)
-    inv_ref[...] = jnp.broadcast_to(inv, (128, 128)).T[0:emb]
-
-    give_scaled.wait()
+    for give in gives:
+        give.wait()
     for dz in range(1, depth):
         to_depth(dz).wait_send()
     for dz in range(depth):
@@ -253,21 +266,20 @@
     chips = groups // 2
     vmem = pl.BlockSpec(memory_space=pltpu.VMEM)
     dma = pltpu.SemaphoreType.DMA
-    scaled, inv, logdeg = pl.pallas_call(
+    return pl.pallas_call(
         functools.partial(kernel, groups, depth),
         out_shape=(
             jax.ShapeDtypeStruct((emb, pix), jnp.float32),
-            jax.ShapeDtypeStruct((emb, 128), jnp.float32),
             jax.ShapeDtypeStruct((1, pix), jnp.float32),
         ),
         in_specs=[pl.BlockSpec(memory_space=pltpu.HBM)] * 4,
-        out_specs=(pl.BlockSpec(memory_space=pltpu.HBM), vmem, vmem),
+        out_specs=(pl.BlockSpec(memory_space=pltpu.HBM), vmem),
         scratch_shapes=[
             pltpu.VMEM((layers, pix), jnp.bfloat16),
             pltpu.VMEM((1, cap), jnp.int32),
             pltpu.VMEM((1, 1), jnp.int32),
             dma((4,)),
-            dma,
+            dma((pix // GIVE,)),
             pltpu.VMEM((chips * depth, 2, emb + AUX + layers, cap), jnp.bfloat16),
             pltpu.VMEM((AUX + layers, pix), jnp.bfloat16),
             pltpu.VMEM((emb + AUX, pix), jnp.float32),
@@ -291,7 +303,6 @@
             transcendentals=pix * cap * groups * depth,
         ),
     )(pixels, landmark_index, counts, factor)
-    return (scaled * inv[:, 0:1], logdeg)
 
 
 def solution(mesh):

time: 33.6 us -> 35.2 us (1.048)
  Pallas kernels: 28.7 us -> 31.2 us
  other arithmetic: 1.95 us -> 0 us
  local copies, waits for them, and re-layouts: 1.47 us -> 2.48 us
    pallas_call x1, Pallas kernels: 28.7 us -> 31.2 us  [per_device(): pl.pallas_call(functools.partial(kernel, groups, depth), out_shape=(jax.S...]
    mul x1 -> x0, other arithmetic: 1.95 us -> none  [per_device(): return (scaled * inv[:, 0:1], logdeg)]
    unnamed x3 -> x4, local copies, waits for them, and re-layouts: 0.6 us -> 2.48 us
    slice x1 -> x0, local copies, waits for them, and re-layouts: 0.86 us -> none  [per_device(): return (scaled * inv[:, 0:1], logdeg)]
where the time goes in v4:
time: 35.2 us; the launch traced here: 35 us
  Pallas kernels  31.2 us (89%)
  local copies, waits for them, and re-layouts  2.48 us (7%)
  between operations  1.29 us (4%)
    pallas_call x1, Pallas kernels, per_device(): pl.pallas_call(functools.partial(kernel, groups, depth), out_shape=(jax.S...  31.2 us
    unnamed x4, local copies, waits for them, and re-layouts  2.48 us

profile of v4, /device:TPU:0, one launch (start us, length us, event | category | flops | bytes accessed | tf_op | source)
XLA Modules:
  0.0 35.0 jit_solution(18020368743243851198)
XLA Ops:
  1.3 31.2 %shard_map.59 = (f32[64,2048]{1,0:T(8,128)}, f32[1,2048]{1,0:T(1,128)}) custom-call(bf16[32,2048]{1,0:T(8,128)(2,1)} %pixels_in.1, s32[1,128]{1,0:T(1,128)} %index_in.1, s32[1,1]{1,0:T(1,128)S(6)} %copy.8.counts_in, bf16[64,128]{1,0:T(8,128)(2,1)} %factor_in.1), custom_call_target="tpu_custom_call" | custom-call | flops 1610612736 | bytes 524288 | tf_op jit(solution)/shard_map/pallas_call | solution.py:269
  32.5 0.0 copy-start
  32.5 1.9 %copy.9 = f32[64,2048]{1,0:T(8,128)} copy(f32[64,2048]{1,0:T(8,128)} %get-tuple-element.4) | data formatting | bytes 1048576
  34.4 0.0 copy-done
  34.4 0.6 %copy.10 = f32[1,2048]{1,0:T(1,128)} copy(f32[1,2048]{1,0:T(1,128)S(1)} %copy-done) | data formatting | bytes 16384
Async XLA Ops:
  32.5 1.9 %copy-start = (f32[1,2048]{1,0:T(1,128)S(1)}, f32[1,2048]{1,0:T(1,128)}, u32[]{:S(2)}) copy-start(f32[1,2048]{1,0:T(1,128)} %get-tuple-element.5) | copy-start | bytes 24580

commit v5 on v3

--- a/solution.py
+++ b/solution.py
@@ -10,7 +10,8 @@
 MESH = pl.DeviceIdType.MESH
 AUX = 16
 CHUNK = 256
-TOGETHER = 3
+TOGETHER = 6
+GIVE = 512
 
 
 def three_way(value):
@@ -124,17 +125,13 @@
             side = jnp.where(prow == put, part, side)
         pix_aug[0:AUX, cols] = side.astype(jnp.bfloat16)
         pix_aug[AUX : AUX + layers, cols] = (own * 0.125).astype(jnp.bfloat16)
-    acc[...] = jnp.zeros_like(acc)
-
-    def absorb(*slots):
-        fac = jnp.concatenate(
-            [blocks[slot, half, 0 : emb + AUX] for slot in slots for half in range(2)], axis=1
-        )
+
+    def absorb(held, first=False):
+        fac = jnp.concatenate([blocks[slot, which, 0 : emb + AUX] for slot, which in held], axis=1)
         side = jnp.concatenate(
             [
-                blocks[slot, half, emb : emb + AUX + layers].astype(jnp.float32).T
-                for slot in slots
-                for half in range(2)
+                blocks[slot, which, emb : emb + AUX + layers].astype(jnp.float32).T
+                for slot, which in held
             ],
             axis=0,
         ).astype(jnp.bfloat16)
@@ -150,13 +147,17 @@
             if at + CHUNK < pix:
                 ahead = exponent(at + CHUNK)
             kern = jnp.exp(expo).astype(jnp.bfloat16)
-            acc[:, at : at + CHUNK] += jnp.dot(fac, kern, preferred_element_type=jnp.float32)
-
-    def bunches(count):
-        return [range(at, min(at + TOGETHER, count)) for at in range(1, count, TOGETHER)]
+            add = jnp.dot(fac, kern, preferred_element_type=jnp.float32)
+            if first:
+                acc[:, at : at + CHUNK] = add
+            else:
+                acc[:, at : at + CHUNK] += add
+
+    def bunches(items):
+        return [items[at : at + TOGETHER] for at in range(0, len(items), TOGETHER)]
 
     arrived(slot_of(0, 0), 1 - core)
-    absorb(slot_of(0, 0))
+    absorb([(slot_of(0, 0), 0), (slot_of(0, 0), 1)], first=True)
 
     def relay(dz, carry):
         slot = slot_of(0, dz)
@@ -176,25 +177,35 @@
 
     lax.fori_loop(1, chips, near, 0)
 
-    for bunch in bunches(depth):
-        for dz in bunch:
-            arrived(slot_of(0, dz), 1 - core)
-        absorb(*[slot_of(0, dz) for dz in bunch])
+    early = [slot_of(0, dz) for dz in range(1, depth)] + [slot_of(dc, 0) for dc in range(1, chips)]
+    for bunch in bunches(early):
+        absorb([(slot, core) for slot in bunch])
+
+    def pass_on(dz):
+        for dc in range(1, chips):
+            slot = slot_of(dc, dz)
+            arrived(slot, core)
+            to_sib(dc, dz).start()
+
+    pass_on(1)
+    for bunch in bunches(early):
+        for slot in bunch:
+            arrived(slot, 1 - core)
+        absorb([(slot, 1 - core) for slot in bunch])
 
     def rest(dz, carry):
         @pl.when(dz + 1 < depth)
         def _():
-            for dc in range(1, chips):
-                arrived(slot_of(dc, dz + 1), core)
-                to_sib(dc, dz + 1).start()
-
-        for bunch in bunches(chips):
-            for dc in bunch:
-                arrived(slot_of(dc, dz), 1 - core)
-            absorb(*[slot_of(dc, dz) for dc in bunch])
-        return carry
-
-    lax.fori_loop(0, depth, rest, 0)
+            pass_on(dz + 1)
+
+        row = [(slot_of(dc, dz), which) for dc in range(1, chips) for which in (core, 1 - core)]
+        for bunch in bunches(row):
+            for slot, which in bunch[1::2]:
+                arrived(slot, which)
+            absorb(bunch)
+        return carry
+
+    lax.fori_loop(1, depth, rest, 0)
 
     part = jnp.zeros((emb, 128), jnp.float32)
     for at in range(0, pix, 128):
@@ -245,6 +256,34 @@
     for dc in range(chips):
         for dz in range(depth):
             to_sib(dc, dz).wait_send()
+
+
+def finish(scaled_in, inv_in, logdeg_in, emb_out, logdeg_out, held, inv_ref, in_sem, out_sem, sems):
+    pix = scaled_in.shape[1]
+    parts = [pl.ds(at, GIVE) for at in range(0, pix, GIVE)]
+    direct = pltpu.make_async_copy(logdeg_in, logdeg_out, sems.at[0])
+    norms = pltpu.make_async_copy(inv_in, inv_ref, sems.at[1])
+    takes = [
+        pltpu.make_async_copy(scaled_in.at[:, part], held.at[:, part], in_sem.at[at])
+        for at, part in enumerate(parts)
+    ]
+    gives = [
+        pltpu.make_async_copy(held.at[:, part], emb_out.at[:, part], out_sem.at[at])
+        for at, part in enumerate(parts)
+    ]
+    norms.start()
+    for take in takes:
+        take.start()
+    direct.start()
+    norms.wait()
+    for at, (take, give) in enumerate(zip(takes, gives)):
+        take.wait()
+        for col in range(at * GIVE, (at + 1) * GIVE, 128):
+            held[:, col : col + 128] = held[:, col : col + 128] * inv_ref[...]
+        give.start()
+    direct.wait()
+    for give in gives:
+        give.wait()
 
 
 def per_device(groups, depth, pixels, landmark_index, counts, factor):
@@ -291,7 +330,27 @@
             transcendentals=pix * cap * groups * depth,
         ),
     )(pixels, landmark_index, counts, factor)
-    return (scaled * inv[:, 0:1], logdeg)
+    hbm = pl.BlockSpec(memory_space=pltpu.HBM)
+    return pl.pallas_call(
+        finish,
+        out_shape=(
+            jax.ShapeDtypeStruct((emb, pix), jnp.float32),
+            jax.ShapeDtypeStruct((1, pix), jnp.float32),
+        ),
+        in_specs=[hbm] * 3,
+        out_specs=(hbm, hbm),
+        scratch_shapes=[
+            pltpu.VMEM((emb, pix), jnp.float32),
+            pltpu.VMEM((emb, 128), jnp.float32),
+            dma((pix // GIVE,)),
+            dma((pix // GIVE,)),
+            dma((2,)),
+        ],
+        compiler_params=pltpu.CompilerParams(vmem_limit_bytes=56 * 1024 * 1024),
+        cost_estimate=pl.CostEstimate(
+            flops=emb * pix, bytes_accessed=8 * emb * pix, transcendentals=0
+        ),
+    )(scaled, inv, logdeg)
 
 
 def solution(mesh):

time: 33.6 us -> 32.1 us (0.955)
  other arithmetic: 1.95 us -> 0 us
  Pallas kernels: 28.7 us -> 30.6 us
  local copies, waits for them, and re-layouts: 1.47 us -> 0 us
    mul x1 -> x0, other arithmetic: 1.95 us -> none  [per_device(): return (scaled * inv[:, 0:1], logdeg)]
    pallas_call x0 -> x1, Pallas kernels: none -> 1.87 us  [per_device(): pl.pallas_call(finish, out_shape=(jax.ShapeDtypeStruct((emb, pix), jnp.fl...]
    slice x1 -> x0, local copies, waits for them, and re-layouts: 0.86 us -> none  [per_device(): return (scaled * inv[:, 0:1], logdeg)]
    unnamed x3 -> x0, local copies, waits for them, and re-layouts: 0.6 us -> none
where the time goes in v5:
time: 32.1 us; the launch traced here: 31.9 us
  Pallas kernels  30.6 us (95%)
  between operations  1.28 us (4%)
    pallas_call x1, Pallas kernels, per_device(): pl.pallas_call(functools.partial(kernel, groups, depth), out_shape=(jax.S...  28.7 us
    pallas_call x1, Pallas kernels, per_device(): pl.pallas_call(finish, out_shape=(jax.ShapeDtypeStruct((emb, pix), jnp.fl...  1.87 us

profile of v5, /device:TPU:0, one launch (start us, length us, event | category | flops | bytes accessed | tf_op | source)
XLA Modules:
  0.0 31.9 jit_solution(14019223075416884036)
XLA Ops:
  1.3 28.7 %shard_map.59 = (f32[64,2048]{1,0:T(8,128)}, f32[64,128]{1,0:T(8,128)}, f32[1,2048]{1,0:T(1,128)}) custom-call(bf16[32,2048]{1,0:T(8,128)(2,1)} %pixels_in.1, s32[1,128]{1,0:T(1,128)} %index_in.1, s32[1,1]{1,0:T(1,128)S(6)} %copy.6.counts_in, bf16[64,128]{1,0:T(8,128)(2,1)} %factor_in.1), custom_call_target="tpu_custom_call" | custom-call | flops 1610612736 | bytes 524288 | tf_op jit(solution)/shard_map/pallas_call | solution.py:295
  30.0 1.9 %shard_map.60 = (f32[64,2048]{1,0:T(8,128)}, f32[1,2048]{1,0:T(1,128)}) custom-call(f32[64,2048]{1,0:T(8,128)} %get-tuple-element.5.scaled_in, f32[64,128]{1,0:T(8,128)} %get-tuple-element.6.inv_in, f32[1,2048]{1,0:T(1,128)} %get-tuple-element.7.logdeg_in), custom_call_target="tpu_custom_call" | custom-call | flops 131072 | bytes 1048576 | tf_op jit(solution)/shard_map/pallas_call | solution.py:334
